TPU v7x, 256 devices: a whole 4x4x8 slice. The times are simulated.
256 devices in a mesh: slot: 4 (over z_hi, core), seq: 64 (over x, y, z_lo).
Axes of the slice: x: 4, y: 4, z: 8 (z_hi: 2, z_lo: 4; z = z_hi * 4 + z_lo), core: 2. Of those that a mesh axis runs over, the one named last changes fastest.
Arguments:
- queries: bfloat16 [4, 2048, 4096], P('slot', 'seq'), may hold values from -100 to 100
- keys: bfloat16 [4, 2048, 4096], P('slot', 'seq'), may hold values from -6 to 6
- values: bfloat16 [4, 2048, 4096], P('slot', 'seq'), may hold values from -6 to 6
- cache_keys: bfloat16 [4, 2048, 4096], P(None, 'seq'), may hold values from -6 to 6
- cache_values: bfloat16 [4, 2048, 4096], P(None, 'seq'), may hold values from -6 to 6
- span_rank: int32 [4], replicated, may hold values from 0 to 3, each once
- noise_level: int32 [4], replicated, may hold values from 0 to 15
- cache_seen: int32 [4], replicated, may hold values from 0 to 4
- gate_table: float32 [16, 32], replicated, may hold values from 0.25 to 2
Outputs:
- shifted: bfloat16 [4, 2048, 4096], P('slot', 'seq')
All inputs are finite; a program needn't handle non-finite values.
Results may differ from a plain program's by a relative error of at most 0.0047.
Values may be sent and summed in bfloat16 or wider, within the bound.
A program may use at most 64 MiB of HBM per device.

v0:
```python
import math

import jax
import jax.numpy as jnp
from jax import lax
from jax.sharding import PartitionSpec as P

HEADS = 32


NEG_FILL = -1e30


def passed_along(value, axis, steps):
    count = lax.axis_size(axis)
    pairs = [(source, (source + steps) % count) for source in range(count)]
    return lax.ppermute(value, axis, pairs)


def attend_block(query_rows, key_rows, value_rows, scale_factor):
    row_count = query_rows.shape[0]
    per_dev = query_rows.shape[1]
    head_dim = query_rows.shape[2]
    block_rows = math.gcd(row_count, 512)
    query_blocks = query_rows.reshape(row_count // block_rows, block_rows, per_dev, head_dim)

    def one_block(query_block):
        scores = (
            jnp.einsum("qhd,khd->hqk", query_block, key_rows, preferred_element_type=jnp.float32)
            * scale_factor
        )
        block_max = jnp.max(scores, axis=-1)
        weights = jnp.exp(scores - block_max[:, :, None])
        block_sum = jnp.sum(weights, axis=-1)
        numerator = jnp.einsum(
            "hqk,khd->qhd",
            weights.astype(jnp.bfloat16),
            value_rows,
            preferred_element_type=jnp.float32,
        )
        return (numerator, block_max.T, block_sum.T)

    numerator, block_max, block_sum = lax.map(one_block, query_blocks)
    return (
        numerator.reshape(row_count, per_dev, head_dim),
        block_max.reshape(row_count, per_dev),
        block_sum.reshape(row_count, per_dev),
    )


def masked_block(query_rows, key_rows, value_rows, scale_factor):
    return attend_block(query_rows, key_rows, value_rows, scale_factor)


def stack_terms(terms):
    return (
        jnp.stack([item[0] for item in terms]),
        jnp.stack([item[1] for item in terms]),
        jnp.stack([item[2] for item in terms]),
    )


def combine_terms(numerators, maxima, sums_all, visible):
    shown = visible[:, None, None]
    top = jnp.max(jnp.where(shown, maxima, NEG_FILL), axis=0)
    coef = jnp.where(shown, jnp.exp(jnp.where(shown, maxima - top[None], 0.0)), 0.0)
    return jnp.sum(coef[:, :, :, None] * numerators, 0) / jnp.sum(coef * sums_all, 0)[:, :, None]


def local(
    queries, keys, values, cache_keys, cache_values, span_rank, noise_level, cache_seen, gate_table
):
    seq_count = lax.axis_size("seq")
    slot_count = lax.axis_size("slot")
    slot_idx = lax.axis_index("slot")
    seq_idx = lax.axis_index("seq")
    tok_rows = queries.shape[1]
    feat_width = queries.shape[2]
    head_dim = feat_width // HEADS
    copies = max(1, seq_count // HEADS)
    per_dev = HEADS * copies // seq_count
    groups = HEADS // per_dev
    half_rows = tok_rows // copies
    lane_width = per_dev * head_dim
    span_tokens = tok_rows * seq_count
    scale_factor = 1.0 / math.sqrt(head_dim)
    query_local = (
        queries[0]
        .reshape(copies, half_rows, groups, lane_width)
        .transpose(1, 2, 0, 3)
        .reshape(half_rows, seq_count, lane_width)
    )
    query_head = lax.all_to_all(query_local, "seq", split_axis=1, concat_axis=0, tiled=True)

    def spread(own, cached):
        paired = lax.dynamic_slice_in_dim(cached, slot_idx, 1, 0)
        stacked = jnp.concatenate([own, paired], 0)
        widened = jnp.broadcast_to(
            stacked.reshape(2, tok_rows, groups, 1, lane_width),
            (2, tok_rows, groups, copies, lane_width),
        )
        return widened.reshape(2, tok_rows, seq_count, lane_width)

    key_head, value_head = (
        lax.all_to_all(spread(keys, cache_keys), "seq", split_axis=2, concat_axis=1, tiled=True),
        lax.all_to_all(
            spread(values, cache_values), "seq", split_axis=2, concat_axis=1, tiled=True
        ),
    )
    slot_range = jnp.arange(slot_count)
    own_rank = jnp.sum(jnp.where(slot_range == slot_idx, span_rank, 0))
    own_level = jnp.sum(jnp.where(slot_range == slot_idx, noise_level, 0))
    own_seen = jnp.sum(jnp.where(slot_range == slot_idx, cache_seen, 0))
    slot_visible = span_rank <= own_rank
    cache_visible = slot_range < own_seen
    key_all, value_all = (
        lax.all_gather(key_head, "slot", axis=0, tiled=True),
        lax.all_gather(value_head, "slot", axis=0, tiled=True),
    )
    key_all = key_all.reshape(slot_count, 2, span_tokens, per_dev, head_dim)
    value_all = value_all.reshape(slot_count, 2, span_tokens, per_dev, head_dim)
    slot_terms = stack_terms(
        [
            masked_block(query_head, key_all[other, 0], value_all[other, 0], scale_factor)
            for other in range(slot_count)
        ]
    )
    cache_terms = stack_terms(
        [
            masked_block(query_head, key_all[cached, 1], value_all[cached, 1], scale_factor)
            for cached in range(slot_count)
        ]
    )
    numerators = jnp.concatenate([slot_terms[0], cache_terms[0]], 0)
    maxima = jnp.concatenate([slot_terms[1], cache_terms[1]], 0)
    sums_all = jnp.concatenate([slot_terms[2], cache_terms[2]], 0)
    total = combine_terms(
        numerators, maxima, sums_all, jnp.concatenate([slot_visible, cache_visible])
    )
    level_onehot = (jnp.arange(gate_table.shape[0]) == own_level).astype(jnp.float32)
    gate_row = jnp.sum(level_onehot[:, None] * gate_table, 0)
    gate_dev = lax.dynamic_slice_in_dim(gate_row, seq_idx // copies * per_dev, per_dev)
    mixed = (gate_dev[None, :, None] * total).astype(jnp.bfloat16)
    sending = mixed.reshape(seq_count, half_rows, 1, lane_width)
    returned = lax.all_to_all(sending, "seq", split_axis=0, concat_axis=2, tiled=True)
    restored = (
        returned.reshape(half_rows, groups, copies, lane_width)
        .transpose(2, 0, 1, 3)
        .reshape(1, tok_rows, feat_width)
    )
    return passed_along(restored, "slot", 1)


def solution(mesh):
    placed = (
        P("slot", "seq", None),
        P("slot", "seq", None),
        P("slot", "seq", None),
        P(None, "seq", None),
        P(None, "seq", None),
        P(),
        P(),
        P(),
        P(),
    )
    return jax.shard_map(
        local, mesh=mesh, in_specs=placed, out_specs=P("slot", "seq", None), check_vma=False
    )
```

profile of v0, /device:TPU:8, one launch (start us, length us, event | category | flops | bytes accessed | tf_op | source)
XLA Modules:
  0.0 310.6 jit_solution(14468049259511042814)
XLA Ops:
  9.0 40.3 %all_to_all.66 = bf16[2,32,64,128]{3,1,0,2:T(8,128)(2,1)S(1)} all-to-all(bf16[2,32,64,128]{3,1,0,2:T(8,128)(2,1)S(1)} %bitcast.425), channel_id=1, replica_groups=mesh['slot'=4,'seq'=64] {'seq'}, dimensions={2} | all-to-all | bytes 2097152 | tf_op jit(solution)/shard_map/all_to_all | solution.py:105
  50.9 78.1 %all_to_all.67 = bf16[2,32,64,128]{3,1,0,2:T(8,128)(2,1)S(1)} all-to-all(bf16[2,32,64,128]{3,1,0,2:T(8,128)(2,1)S(1)} %bitcast.426), channel_id=1, replica_groups=mesh['slot'=4,'seq'=64] {'seq'}, dimensions={2} | all-to-all | bytes 2097152 | tf_op jit(solution)/shard_map/all_to_all | solution.py:106
  131.1 5.5 %all-to-all-start = ((bf16[16,64,128]{2,0,1:T(8,128)(2,1)}), bf16[16,64,128]{2,0,1:T(8,128)(2,1)S(1)}, u32[]{:S(2)}, u32[]{:S(2)}) async-start(bf16[16,64,128]{2,0,1:T(8,128)(2,1)} %bitcast.74), calls=%async_computation | async-start | bytes 524288 | tf_op jit(solution)/shard_map/all_to_all | solution.py:93
  141.6 3.8 %slice_bitcast_fusion.1 = (bf16[2048,1,128]{2,0,1:T(8,128)(2,1)S(1)}, bf16[2048,1,128]{2,0,1:T(8,128)(2,1)S(1)}, bf16[2048,1,128]{2,0,1:T(8,128)(2,1)S(1)}, bf16...) fusion(bf16[4,2,2048,1,128]{4,2,3,1,0:T(8,128)(2,1)} %bitcast.421), kind=kLoop, calls=%fused_computation.148 | loop fusion | bytes 8388608 | tf_op jit(solution)/shard_map/squeeze | solution.py:130
  145.4 48.2 %all-gather.5.cloned.1.call-done = bf16[8,2048,1,128]{3,1,2,0:T(8,128)(2,1)} async-done(((bf16[2,2048,1,128]{3,1,2,0:T(8,128)(2,1)}), bf16[8,2048,1,128]{3,1,2,0:T(8,128)(2,1)}) %all-gather.5.cloned.1.call-update) | async-done | bytes 4194320 | tf_op jit(solution)/shard_map/all_gather | solution.py:118
  193.6 3.7 %slice_bitcast_fusion = (bf16[2048,1,128]{2,0,1:T(8,128)(2,1)S(1)}, bf16[2048,1,128]{2,0,1:T(8,128)(2,1)S(1)}, bf16[2048,1,128]{2,0,1:T(8,128)(2,1)S(1)}, bf16[2...) fusion(bf16[4,2,2048,1,128]{4,2,3,1,0:T(8,128)(2,1)} %bitcast.422), kind=kLoop, calls=%fused_computation.147 | loop fusion | bytes 8388608 | tf_op jit(solution)/shard_map/squeeze | solution.py:130
  198.1 8.6 %while.113 = (s32[]{:T(128)}, f32[2,512,1,128]{3,1,2,0:T(8,128)}, f32[2,512,1]{1,2,0:T(1,128)S(1)}, f32[2,512,1]{1,2,0:T(1,128)S(1)}, bf16[2,512,1,128]{3,1,2,0:...) while((s32[]{:T(128)}, f32[2,512,1,128]{3,1,2,0:T(8,128)}, ...), condition=%wide.region_11.12_spmd, body=%wide.region_8.11_spmd.sunk | while | flops 545258496 | bytes 16138873 | solution.py:43
  198.1 1.9 multiply_reduce_fusion.19
  207.6 8.6 %while.112 = (s32[]{:T(128)}, f32[2,512,1,128]{3,1,2,0:T(8,128)}, f32[2,512,1]{1,2,0:T(1,128)S(1)}, f32[2,512,1]{1,2,0:T(1,128)S(1)}, bf16[2,512,1,128]{3,1,2,0:...) while((s32[]{:T(128)}, f32[2,512,1,128]{3,1,2,0:T(8,128)}, ...), condition=%wide.region_7.8_spmd, body=%wide.region_4.7_spmd.sunk | while | flops 545258496 | bytes 16138873 | solution.py:43
  207.6 1.9 multiply_reduce_fusion.18
  211.8 1.9 multiply_reduce_fusion.18
  217.0 8.6 %while.114 = (s32[]{:T(128)}, f32[2,512,1,128]{3,1,2,0:T(8,128)}, f32[2,512,1]{1,2,0:T(1,128)S(1)}, f32[2,512,1]{1,2,0:T(1,128)S(1)}, bf16[2,512,1,128]{3,1,2,0:...) while((s32[]{:T(128)}, f32[2,512,1,128]{3,1,2,0:T(8,128)}, ...), condition=%wide.region_15.16_spmd, body=%wide.region_12.15_spmd.sunk | while | flops 545258496 | bytes 16138873 | solution.py:43
  217.0 1.9 multiply_reduce_fusion.20
  221.3 1.9 multiply_reduce_fusion.20
  226.4 8.6 %while.115 = (s32[]{:T(128)}, f32[2,512,1,128]{3,1,2,0:T(8,128)}, f32[2,512,1]{1,2,0:T(1,128)S(1)}, f32[2,512,1]{1,2,0:T(1,128)S(1)}, bf16[2,512,1,128]{3,1,2,0:...) while((s32[]{:T(128)}, f32[2,512,1,128]{3,1,2,0:T(8,128)}, ...), condition=%wide.region_19.20_spmd, body=%wide.region_16.19_spmd.sunk | while | flops 545258496 | bytes 16138873 | solution.py:43
  226.4 1.9 multiply_reduce_fusion.21
  230.7 1.9 multiply_reduce_fusion.21
  235.9 8.6 %while.116 = (s32[]{:T(128)}, f32[2,512,1,128]{3,1,2,0:T(8,128)}, f32[2,512,1]{1,2,0:T(1,128)S(1)}, f32[2,512,1]{1,2,0:T(1,128)S(1)}, bf16[2,512,1,128]{3,1,2,0:...) while((s32[]{:T(128)}, f32[2,512,1,128]{3,1,2,0:T(8,128)}, ...), condition=%wide.region_23.24_spmd, body=%wide.region_20.23_spmd.sunk | while | flops 545258496 | bytes 16138873 | solution.py:43
  235.9 1.9 multiply_reduce_fusion.22
  245.3 6.3 %while.117 = (s32[]{:T(128)}, f32[2,512,1,128]{3,1,2,0:T(8,128)}, f32[2,512,1]{1,2,0:T(1,128)S(1)}, f32[2,512,1]{1,2,0:T(1,128)S(1)}, bf16[2,512,1,128]{3,1,2,0:...) while((s32[]{:T(128)}, f32[2,512,1,128]{3,1,2,0:T(8,128)}, ...), condition=%wide.region_27.28_spmd, body=%wide.region_24.27_spmd.sunk | while | flops 545258496 | bytes 14041693 | solution.py:43
  251.7 5.0 %while.118 = (s32[]{:T(128)}, f32[2,512,1,128]{3,1,2,0:T(8,128)S(1)}, f32[2,512,1]{1,2,0:T(1,128)S(1)}, f32[2,512,1]{1,2,0:T(1,128)S(1)}, bf16[2,512,1,128]{3,1,...) while((s32[]{:T(128)}, ...), condition=%wide.region_31.32_spmd, body=%wide.region_28.31_spmd.sunk | while | flops 545258496 | bytes 14041185 | solution.py:43
  256.8 5.0 %while.119 = (s32[]{:T(128)}, f32[2,512,1,128]{3,1,2,0:T(8,128)S(1)}, f32[2,512,1]{1,2,0:T(1,128)S(1)}, f32[2,512,1]{1,2,0:T(1,128)S(1)}, bf16[2,512,1,128]{3,1,...) while((s32[]{:T(128)}, ...), condition=%wide.region_35.36_spmd, body=%wide.region_32.35_spmd.sunk | while | flops 545258496 | bytes 14041185 | solution.py:43
  271.3 20.3 %all_to_all.68 = bf16[64,16,1,128]{3,1,2,0:T(8,128)(2,1)S(1)} all-to-all(bf16[64,16,1,128]{3,1,2,0:T(8,128)(2,1)S(1)} %multiply_convert_fusion), channel_id=1, replica_groups=mesh['slot'=4,'seq'=64] {'seq'}, dimensions={0} | all-to-all | bytes 524288 | tf_op jit(solution)/shard_map/all_to_all | solution.py:145
  291.9 11.2 %collective-permute-done = bf16[1,32,4096]{2,1,0:T(8,128)(2,1)S(1)} collective-permute-done((bf16[1,32,4096]{2,1,0:T(8,128)(2,1)S(1)}, bf16[1,32,4096]{2,1,0:T(8,128)(2,1)S(1)}, u32[]{:S(2)}, u32[]{:S(2)}) %collective-permute-start) | collective-permute-done | bytes 262176 | tf_op jit(solution)/shard_map/ppermute | solution.py:17
  (172 shorter events, 70.4 us)
Async XLA Ops:
  6.5 135.1 %all-gather.3.cloned.1.call-start = ((), (), s32[]{:S(2)}) async-start(), calls=%async_computation.4 | async-start | bytes 5242880 | tf_op jit(solution)/shard_map/all_gather | solution.py:117
  7.6 42.9 %copy-start.6 = (bf16[1,32,4096]{2,1,0:T(8,128)(2,1)S(1)}, bf16[1,32,4096]{2,1,0:T(8,128)(2,1)}, u32[]{:S(2)}) copy-start(bf16[1,32,4096]{2,1,0:T(8,128)(2,1)} %param.27) | copy-start | bytes 786436
  50.4 79.8 %copy-start.5 = (bf16[1,32,4096]{2,1,0:T(8,128)(2,1)S(1)}, bf16[1,32,4096]{2,1,0:T(8,128)(2,1)}, u32[]{:S(2)}) copy-start(bf16[1,32,4096]{2,1,0:T(8,128)(2,1)} %param.25) | copy-start | bytes 786436
  50.4 143.1 %all-gather.5.cloned.1.call-start = ((), (), s32[]{:S(2)}) async-start(), calls=%async_computation.5 | async-start | bytes 5242880 | tf_op jit(solution)/shard_map/all_gather | solution.py:118
  50.6 86.1 %copy-start.11 = (s32[4]{0:T(128)S(1)}, s32[4]{0:T(128)}, u32[]{:S(2)}) copy-start(s32[4]{0:T(128)} %param.31) | copy-start | bytes 52
  50.6 87.5 %copy-start.7 = (f32[16,32]{1,0:T(8,128)S(1)}, f32[16,32]{1,0:T(8,128)}, u32[]{:S(2)}) copy-start(f32[16,32]{1,0:T(8,128)} %param.33) | copy-start | bytes 6148
  50.6 88.2 %copy-start.9 = (s32[4]{0:T(128)S(1)}, s32[4]{0:T(128)}, u32[]{:S(2)}) copy-start(s32[4]{0:T(128)} %param.32) | copy-start | bytes 52
  50.6 88.2 %copy-start.10 = (s32[4]{0:T(128)S(1)}, s32[4]{0:T(128)}, u32[]{:S(2)}) copy-start(s32[4]{0:T(128)} %param.30) | copy-start | bytes 52
  131.1 66.1 %all-to-all-start = ((bf16[16,64,128]{2,0,1:T(8,128)(2,1)}), bf16[16,64,128]{2,0,1:T(8,128)(2,1)S(1)}, u32[]{:S(2)}, u32[]{:S(2)}) async-start(bf16[16,64,128]{2,0,1:T(8,128)(2,1)} %bitcast.74), calls=%async_computation | async-start | bytes 524288 | tf_op jit(solution)/shard_map/all_to_all | solution.py:93
  198.1 2.7 copy-start.4
  202.4 2.7 copy-start.4
  207.6 2.7 copy-start.3
  211.8 2.7 copy-start.3
  217.0 2.7 copy-start.2
  221.3 2.7 copy-start.2
  226.4 2.7 copy-start.1
  230.7 2.7 copy-start.1
  235.9 2.7 copy-start
  240.2 2.7 copy-start
  256.8 5.2 %copy-start.8 = (pred[8]{0:T(512)(128)(4,1)S(1)}, pred[8]{0:T(512)(128)(4,1)}, u32[]{:S(2)}) copy-start(pred[8]{0:T(512)(128)(4,1)} %pad_add_fusion) | copy-start | bytes 28
  291.8 11.3 %collective-permute-start = (bf16[1,32,4096]{2,1,0:T(8,128)(2,1)S(1)}, bf16[1,32,4096]{2,1,0:T(8,128)(2,1)S(1)}, u32[]{:S(2)}, u32[]{:S(2)}) collective-permute-start(bf16[1,32,4096]{2,1,0:T(8,128)(2,1)S(1)} %reshape.1068), channel_id=1, source_target_pairs={{0,64},{64,128},{128,192},{192,0},{1,65},{65,129},{129,193},{193,1... | collective-permute-start | bytes 786440 | tf_op jit(solution)/shard_map/ppermute | solution.py:17
Sparse Core Ops, SparseCore 0:
  50.5 72.8 all-gather.2
  130.4 63.1 all-gather.4
where the time goes:
time: 312 us; the launch traced here: 311 us
  blocking collectives  139 us (45%)
  waiting for transfers between devices  59.4 us (19%)
  matrix products  45.6 us (15%)
  local copies, waits for them, and re-layouts  26 us (8%)
  other arithmetic  21.2 us (7%)
  between operations  13.8 us (4%)
  starting transfers between devices  5.64 us (2%)
    all_to_all x1, blocking collectives, local(): lax.all_to_all(spread(values, cache_values), 'seq', split_axis=2, concat_...  78.1 us
    all_gather x1, waiting for transfers between devices, local(): lax.all_gather(value_head, 'slot', axis=0, tiled=True)  48.2 us
    all_to_all x1, blocking collectives, local(): lax.all_to_all(spread(keys, cache_keys), 'seq', split_axis=2, concat_axis...  40.3 us
    dot_general x16, matrix products, one_block(): jnp.einsum('qhd,khd->hqk', query_block, key_rows, preferred_element_type=...  23.6 us
    dot_general x16, matrix products, one_block(): jnp.einsum('hqk,khd->qhd', weights.astype(jnp.bfloat16), value_rows, pref...  22 us
    all_to_all x1, blocking collectives, local(): lax.all_to_all(sending, 'seq', split_axis=0, concat_axis=2, tiled=True)  20.3 us
    reduce_sum x16, other arithmetic, one_block(): block_sum = jnp.sum(weights, axis=-1)  13.2 us
    ppermute x1, waiting for transfers between devices, passed_along(): return lax.ppermute(value, axis, pairs)  11.2 us
  transfers between devices with their start and end apart: 4, of which 2 were waited for; matrix products, arithmetic and copies ran while one was open for 5% of the time, Pallas kernels for 0%

commit v1 on v0

v1 whole, which is shorter than its diff:
```python
import functools
import math

import jax
import jax.numpy as jnp
from jax import lax
from jax.experimental import pallas as pl
from jax.experimental.pallas import tpu as pltpu
from jax.sharding import PartitionSpec as P

HEADS = 32
HD = 128
ROWS = 32
NX, NY, NZ = 4, 4, 8
MESH = pl.DeviceIdType.MESH
BF = jnp.bfloat16
NEG = -1e30


def place():
    slot, seq = lax.axis_index("slot"), lax.axis_index("seq")
    return seq // 16, (seq // 4) % 4, (slot // 2) * 4 + seq % 4, slot % 2


def device(x, y, z, core):
    return ((z // 4) * 2 + core, x * 16 + y * 4 + z % 4)


def wait_bytes(ref, sem):
    pltpu.make_async_copy(ref, ref, sem).wait()


def greet(peers):
    barrier = pltpu.get_barrier_semaphore()
    for peer in peers:
        pl.semaphore_signal(barrier, inc=1, device_id=peer, device_id_type=MESH)
    pl.semaphore_wait(barrier, len(peers))


def remote(src, dst, send, recv, peer):
    pltpu.make_async_remote_copy(
        src_ref=src, dst_ref=dst, send_sem=send, recv_sem=recv, device_id=peer, device_id_type=MESH
    ).start()


def gather_kernel(
    q_ref, k_ref, v_ref, ck_ref, cv_ref, qb, kb, vb,
    sq, sk, sv, sck, scv,
    y_send, y_recv, z_send, z_recv, x_send, x_recv, s_send, s_recv,
):
    x, y, z, c = place()
    zl, zhi = z % 4, z // 4
    odd = z % 2
    q_core = c + odd - 2 * c * odd
    step = 1 - 2 * c
    ahead = device((x + step + NX) % NX, y, z, c)
    behind = device((x - step + NX) % NX, y, z, c)
    other = device(x, y, z, 1 - c)

    peers = [device(x, (y + d) % NY, z, c) for d in range(1, NY)]
    peers += [device(x, y, (z + d) % NZ, c) for d in range(1, NZ)]
    peers += [device(x, y, (z + d) % NZ, 1 - c) for d in range(NZ)]
    peers += [ahead, behind]
    greet(peers)

    pairs = [((z // 2 + e - c + 4) % 4) for e in range(2)]

    def y_cached(ref, held, n):
        for d in (1, 2, 3, 0):
            to = (y + d) % NY
            for e in range(2):
                src = ref.at[pl.ds(2 * c, 2), :, pl.ds(pl.multiple_of(to * 1024 + pairs[e] * 256, 256), 256)]
                dst = held.at[e, :, y]
                if d:
                    remote(src, dst, y_send.at[n], y_recv.at[n], device(x, to, z, c))
                else:
                    pltpu.make_async_copy(src, dst, y_recv.at[n]).start()

    def y_own(ref, held, n):
        for d in (1, 2, 3, 0):
            to = (y + d) % NY
            src = ref.at[0, :, pl.ds(pl.multiple_of(to * 1024, 1024), 1024)]
            dst = held.at[y]
            if d:
                remote(src, dst, y_send.at[n], y_recv.at[n], device(x, to, z, c))
            else:
                pltpu.make_async_copy(src, dst, y_recv.at[n]).start()

    def z_cached(held, out, n):
        wait_bytes(held, y_recv.at[n])
        for e in range(2):
            for w in range(2):
                to = pairs[e] * 2 + w
                src = held.at[e, :, :, :, pl.ds(w * 128, 128)]
                dst = out.at[0, 0, pl.ds(2, 2), zl]

                @pl.when(to == z)
                def _():
                    pltpu.make_async_copy(src, dst, z_recv.at[n]).start()

                @pl.when(to != z)
                def _():
                    remote(src, dst, z_send.at[n], z_recv.at[n], device(x, y, to, c))

    def z_own(held, out, n):
        wait_bytes(held, y_recv.at[n])
        for d in (4, 3, 5, 2, 6, 1, 7, 0):
            to = (z + d) % NZ
            src = held.at[:, :, pl.ds(pl.multiple_of(to * 128, 128), 128)]
            dst = out.at[0, 0, zhi, zl]
            if d:
                remote(src, dst, z_send.at[n], z_recv.at[n], device(x, y, to, c))
            else:
                pltpu.make_async_copy(src, dst, z_recv.at[n]).start()

    def z_query(n):
        wait_bytes(sq, y_recv.at[n])
        dst = qb.at[zhi * 2 + c, zl // 2]
        for d in (4, 3, 5, 2, 6, 1, 7, 0):
            to = (z + d) % NZ
            src = sq.at[:, :, pl.ds(pl.multiple_of(to * 128, 128), 128)]
            if d:
                remote(src, dst, z_send.at[n], z_recv.at[n], device(x, y, to, q_core))
            else:

                @pl.when(odd == 0)
                def _():
                    pltpu.make_async_copy(src, dst, z_recv.at[n]).start()

                @pl.when(odd == 1)
                def _():
                    remote(src, dst, z_send.at[n], z_recv.at[n], other)

    def unit(out, n, j, owner=0):
        return out.at[owner, j, pl.ds(2, 2) if n < 2 else pl.ds(0, 2)]

    def share(out, n, j):
        remote(unit(out, n, j), unit(out, n, j, 1), s_send.at[n, j], s_recv.at[n, j], other)

    def x0(out, n):
        wait_bytes(unit(out, n, 0), z_recv.at[n])
        remote(unit(out, n, 0), unit(out, n, 1), x_send.at[n, 0], x_recv.at[n, 0], ahead)
        remote(unit(out, n, 0), unit(out, n, 3), x_send.at[n, 1], x_recv.at[n, 1], behind)
        share(out, n, 0)

    def x1(out, n):
        wait_bytes(unit(out, n, 1), x_recv.at[n, 0])
        remote(unit(out, n, 1), unit(out, n, 2), x_send.at[n, 2], x_recv.at[n, 2], ahead)
        share(out, n, 1)
        wait_bytes(unit(out, n, 3), x_recv.at[n, 1])
        share(out, n, 3)

    def x2(out, n):
        wait_bytes(unit(out, n, 2), x_recv.at[n, 2])
        share(out, n, 2)

    CK, CV, K, V, Q = range(5)
    y_cached(ck_ref, sck, CK)
    y_cached(cv_ref, scv, CV)
    y_own(q_ref, sq, Q)
    y_own(k_ref, sk, K)
    y_own(v_ref, sv, V)
    z_cached(sck, kb, CK)
    z_cached(scv, vb, CV)
    z_query(Q)
    x0(kb, CK)
    z_own(sk, kb, K)
    x0(vb, CV)
    z_own(sv, vb, V)
    x1(kb, CK)
    x0(kb, K)
    x1(vb, CV)
    x2(kb, CK)
    x0(vb, V)
    x2(vb, CV)
    x1(kb, K)
    x1(vb, V)
    x2(kb, K)
    x2(vb, V)

    wait_bytes(sq, z_recv.at[Q])
    for n, out in ((CK, kb), (CV, vb), (K, kb), (V, vb)):
        for j in range(4):
            wait_bytes(unit(out, n, j, 1), s_recv.at[n, j])
            wait_bytes(unit(out, n, j), s_send.at[n, j])
        for j in range(3):
            wait_bytes(unit(out, n, j), x_send.at[n, j])
    for n, held in ((Q, sq), (K, sk), (V, sv)):
        wait_bytes(held.at[pl.ds(0, 3)], y_send.at[n])
    for n, held in ((CK, sck), (CV, scv)):
        wait_bytes(held.at[:, :, pl.ds(0, 3)], y_send.at[n])
        wait_bytes(held.at[:, :, pl.ds(0, 3)], z_send.at[n])
    for n, held in ((K, sk), (V, sv)):
        wait_bytes(held.at[:, :, pl.ds(0, 896)], z_send.at[n])

    @pl.when(odd == 0)
    def _():
        wait_bytes(sq.at[:, :, pl.ds(0, 896)], z_send.at[Q])

    @pl.when(odd == 1)
    def _():
        wait_bytes(sq, z_send.at[Q])


def gather(q, k, v, ck, cv):
    dma = pltpu.SemaphoreType.DMA
    return pl.pallas_call(
        gather_kernel,
        out_shape=(
            jax.ShapeDtypeStruct((4, 2, NY, ROWS, HD), BF),
            jax.ShapeDtypeStruct((2, NX, 4, 4, NY, ROWS, HD), BF),
            jax.ShapeDtypeStruct((2, NX, 4, 4, NY, ROWS, HD), BF),
        ),
        in_specs=[pl.BlockSpec(memory_space=pl.ANY)] * 5,
        out_specs=[pl.BlockSpec(memory_space=pl.ANY)] * 3,
        scratch_shapes=[
            pltpu.VMEM((NY, ROWS, 1024), BF),
            pltpu.VMEM((NY, ROWS, 1024), BF),
            pltpu.VMEM((NY, ROWS, 1024), BF),
            pltpu.VMEM((2, 2, NY, ROWS, 256), BF),
            pltpu.VMEM((2, 2, NY, ROWS, 256), BF),
            dma((5,)), dma((5,)), dma((5,)), dma((5,)),
            dma((4, 3)), dma((4, 3)), dma((4, 4)), dma((4, 4)),
        ],
        compiler_params=pltpu.CompilerParams(
            collective_id=0, has_side_effects=True, vmem_limit_bytes=16 * 2**20
        ),
        name="gather",
    )(q, k, v, ck, cv)


def attend_kernel(rank, level, seen, where, gate, q_ref, k_ref, v_ref, o_ref, acc, top, den):
    blk = pl.program_id(0)
    core, head = where[0], where[1]
    owner, i = blk // 4, blk % 4
    holder = jnp.where(owner == 0, core, 1 - core)
    scale = math.log2(math.e) / math.sqrt(HD)

    @pl.when(blk == 0)
    def _():
        acc[...] = jnp.zeros_like(acc)
        den[...] = jnp.zeros_like(den)
        top[...] = jnp.full_like(top, NEG)

    for s in range(4):
        in_flight = rank[jnp.where(i < 2, 2 * i + holder, 0)] <= rank[s]
        cached = 2 * holder + i - 2 < seen[s]
        visible = jnp.where(i < 2, in_flight, cached)

        @pl.when(visible)
        def _():
            scores = lax.dot_general(
                q_ref[s], k_ref[0, :, 0].reshape(2048, HD), (((1,), (1,)), ((), ())),
                preferred_element_type=jnp.float32,
            )
            old = top[s, :, :1]
            new = jnp.maximum(old, jnp.max(scores, axis=1, keepdims=True))
            weights = jnp.exp2(scores * scale - new * scale)
            fade = jnp.exp2((old - new) * scale)
            den[s] = den[s] * fade + jnp.sum(weights, axis=1, keepdims=True)
            acc[s] = acc[s] * fade + jnp.dot(
                weights.astype(BF), v_ref[0, :, 0].reshape(2048, HD),
                preferred_element_type=jnp.float32,
            )
            top[s] = jnp.broadcast_to(new, top.shape[1:])

    @pl.when(blk == 7)
    def _():
        for s in range(4):
            o_ref[s] = (gate[level[s], head] * (acc[s] / den[s])).astype(BF)


def attend(rank, level, seen, where, gate, q, k, v):
    smem = pl.BlockSpec(memory_space=pltpu.SMEM)
    block = pl.BlockSpec((1, NX, 1, 512, HD), lambda b: (b // 4, 0, b % 4, 0, 0))
    whole = pl.BlockSpec((4, 256, HD), lambda b: (0, 0, 0))
    return pl.pallas_call(
        attend_kernel,
        grid=(8,),
        out_shape=jax.ShapeDtypeStruct((4, 256, HD), BF),
        in_specs=[smem] * 5 + [whole, block, block],
        out_specs=whole,
        scratch_shapes=[
            pltpu.VMEM((4, 256, HD), jnp.float32),
            pltpu.VMEM((4, 256, HD), jnp.float32),
            pltpu.VMEM((4, 256, HD), jnp.float32),
        ],
        compiler_params=pltpu.CompilerParams(vmem_limit_bytes=40 * 2**20),
        name="attend",
    )(rank, level, seen, where, gate, q, k, v)


def return_kernel(a_ref, o_ref, held, y_send, y_recv, z_send, z_recv):
    x, y, z, c = place()
    peers = [device(x, (y + d) % NY, z, c) for d in range(1, NY)]
    peers += [device(x, y, (z + d) % NZ, c) for d in range(1, NZ)]
    peers += [device(x, y, (z + d) % NZ, 1 - c) for d in range(NZ)]
    greet(peers)

    for d in (4, 3, 5, 2, 6, 1, 7, 0):
        to = (z + d) % NZ
        odd = to % 2
        core = 1 - (c + odd - 2 * c * odd)
        span = (2 * (to // 4) + core + 3) % 4
        src = a_ref.at[span, (to % 4) // 2]
        dst = held.at[:, :, pl.ds(pl.multiple_of(z * 128, 128), 128)]
        if d:
            remote(src, dst, z_send, z_recv, device(x, y, to, core))
        else:

            @pl.when(odd == 1)
            def _():
                pltpu.make_async_copy(src, dst, z_recv).start()

            @pl.when(odd == 0)
            def _():
                remote(src, dst, z_send, z_recv, device(x, y, z, 1 - c))

    wait_bytes(held, z_recv)
    for d in (2, 1, 3, 0):
        to = (y + d) % NY
        src = held.at[to]
        dst = o_ref.at[0, :, pl.ds(pl.multiple_of(y * 1024, 1024), 1024)]
        if d:
            remote(src, dst, y_send, y_recv, device(x, to, z, c))
        else:
            pltpu.make_async_copy(src, dst, y_recv).start()
    wait_bytes(o_ref, y_recv)
    wait_bytes(held.at[pl.ds(0, 3)], y_send)

    @pl.when(z % 2 == 1)
    def _():
        wait_bytes(held.at[:, :, pl.ds(0, 896)], z_send)

    @pl.when(z % 2 == 0)
    def _():
        wait_bytes(held, z_send)


def send_back(a):
    dma = pltpu.SemaphoreType.DMA
    return pl.pallas_call(
        return_kernel,
        out_shape=jax.ShapeDtypeStruct((1, ROWS, HEADS * HD), BF),
        in_specs=[pl.BlockSpec(memory_space=pl.ANY)],
        out_specs=pl.BlockSpec(memory_space=pl.ANY),
        scratch_shapes=[pltpu.VMEM((NY, ROWS, 1024), BF), dma, dma, dma, dma],
        compiler_params=pltpu.CompilerParams(
            collective_id=1, has_side_effects=True, vmem_limit_bytes=16 * 2**20
        ),
        name="send_back",
    )(a)


def local(q, k, v, ck, cv, rank, level, seen, gate):
    qb, kb, vb = gather(q, k, v, ck, cv)
    _, y, z, c = place()
    where = jnp.stack([c, y * NZ + z]).astype(jnp.int32)
    mixed = attend(
        rank, level, seen, where, gate,
        qb.reshape(4, 256, HD), kb.reshape(2, NX, 4, 512, HD), vb.reshape(2, NX, 4, 512, HD),
    )
    return send_back(mixed.reshape(4, 2, NY, ROWS, HD))


def solution(mesh):
    own, cached = P("slot", "seq", None), P(None, "seq", None)
    placed = (own, own, own, cached, cached, P(), P(), P(), P())
    return jax.shard_map(local, mesh=mesh, in_specs=placed, out_specs=own, check_vma=False)
```

time: 312 us -> 110 us (0.35)
  blocking collectives: 139 us -> 0 us
  Pallas kernels: 0 us -> 99.5 us
  waiting for transfers between devices: 59.4 us -> 0 us
  matrix products: 45.6 us -> 0 us
  other arithmetic: 21.2 us -> 0.07 us
  local copies, waits for them, and re-layouts: 26 us -> 8.66 us
  between operations: 13.8 us -> 0.04 us
  starting transfers between devices: 5.64 us -> 0 us
    all_to_all x3 -> x0, blocking collectives: 139 us -> none  [the longest x1 78.1 us: local(): lax.all_to_all(spread(values, cache_values), 'seq', split_axis=2, concat_...]
    pallas_call x0 -> x3, Pallas kernels: none -> 99.5 us  [the longest x1 61.6 us: gather(): pl.pallas_call(gather_kernel, out_shape=(jax.ShapeDtypeStruct((4, 2, NY,...]
    all_gather x2 -> x0, waiting for transfers between devices: 48.2 us -> none  [the longest x1 48.2 us: local(): lax.all_gather(value_head, 'slot', axis=0, tiled=True)]
    dot_general x32 -> x0, matrix products: 45.6 us -> none  [the longest x16 23.6 us: one_block(): jnp.einsum('qhd,khd->hqk', query_block, key_rows, preferred_element_type=...]
    reduce_sum x21 -> x0, other arithmetic: 16.2 us -> none  [the longest x16 13.2 us: one_block(): block_sum = jnp.sum(weights, axis=-1)]
    ppermute x1 -> x0, waiting for transfers between devices: 11.2 us -> none  [passed_along(): return lax.ppermute(value, axis, pairs)]
    squeeze x2 -> x0, local copies, waits for them, and re-layouts: 7.47 us -> none  [the longest x1 3.8 us: local(): key_all[cached, 1]]
    another operation x25 -> x0, local copies, waits for them, and re-layouts: 5.99 us -> none
  transfers between devices with their start and end apart: 4 -> 0, of which waited for: 2 -> 0; matrix products, arithmetic and copies ran while one was open for 5% -> 0% of each run, Pallas kernels for 0% -> 0%
where the time goes in v1:
time: 110 us; the launch traced here: 108 us
  Pallas kernels  99.5 us (90%)
  local copies, waits for them, and re-layouts  8.66 us (8%)
    pallas_call x1, Pallas kernels, gather(): pl.pallas_call(gather_kernel, out_shape=(jax.ShapeDtypeStruct((4, 2, NY,...  61.6 us
    pallas_call x1, Pallas kernels, attend(): pl.pallas_call(attend_kernel, grid=(8,), out_shape=jax.ShapeDtypeStruct((...  20.1 us
    pallas_call x1, Pallas kernels, send_back(): pl.pallas_call(return_kernel, out_shape=jax.ShapeDtypeStruct((1, ROWS, HE...  17.8 us
    unnamed x19, local copies, waits for them, and re-layouts  8.66 us

profile of v1, /device:TPU:8, one launch (start us, length us, event | category | flops | bytes accessed | tf_op | source)
XLA Modules:
  0.0 108.3 jit_solution(14397619807710255303)
XLA Ops:
  0.0 0.1 pad_add_fusion.where
  0.1 0.0 copy-start
  0.1 1.2 %copy-done = bf16[4,32,4096]{2,1,0:T(8,128)(2,1)S(1)} copy-done((bf16[4,32,4096]{2,1,0:T(8,128)(2,1)S(1)}, bf16[4,32,4096]{2,1,0:T(8,128)(2,1)}, u32[]{:S(2)}) %copy-start) | copy-done | bytes 1048600
  1.3 0.0 copy-start.1
  1.3 1.2 %copy-done.1 = bf16[4,32,4096]{2,1,0:T(8,128)(2,1)S(1)} copy-done((bf16[4,32,4096]{2,1,0:T(8,128)(2,1)S(1)}, bf16[4,32,4096]{2,1,0:T(8,128)(2,1)}, u32[]{:S(2)}) %copy-start.1) | copy-done | bytes 1048600
  2.5 0.0 copy-start.2
  2.5 0.9 copy-done.2
  3.5 0.0 copy-start.3
  3.5 0.9 copy-done.3
  4.4 0.0 copy-start.4
  4.4 0.9 copy-done.4
  5.4 61.6 %gather.1 = (bf16[4,2,4,32,128]{4,3,2,1,0:T(8,128)(2,1)S(1)}, bf16[2,4,4,4,4,32,128]{6,5,4,3,2,1,0:T(8,128)(2,1)S(1)}, bf16[2,4,4,4,4,32,128]{6,5,4,3,2,1,0:T(8,128)(2,1)S(1)}) custom-call(bf16[1,32,4096]{2,1,0:T(8,128)(2,1)S(1)} %copy-done.2, bf16[1,32,4096]{2,1,0:T(8,128)(2,1)S(1)} %copy-done.3, bf16[1,32,4096]{2,1,0:T(8,128)(2,1)S(1)} %copy-done.4, ...), custom_call_target="tpu_custom_call" | custom-call | tf_op jit(solution)/shard_map/gather/pallas_call | solution.py:207
  67.0 0.0 copy-start.5
  67.0 0.7 copy-done.5
  67.7 0.0 copy-start.6
  67.7 0.7 copy-done.6
  68.3 0.0 copy-start.7
  68.3 0.7 copy-done.7
  69.0 0.0 copy-start.8
  69.0 0.7 copy-done.8
  69.6 20.1 %attend.1 = bf16[4,256,128]{2,1,0:T(8,128)(2,1)S(1)} custom-call(s32[4]{0:T(128)S(1)} %copy-done.6, s32[4]{0:T(128)S(1)} %copy-done.7, s32[4]{0:T(128)S(1)} %copy-done.8, s32[2]{0:T(128)S(1)} %pad_add_fusion.where, f32[16,32]{1,0:T(8,128)S(1)} %copy-done.5, bf16[4,256,128]{2,1,0:T(8,128)(2,1)S(1)} %bitcast.9, bf16[2,4,4,512,128]{4,3,2,1,0:T(8,128)(2,1)S(1)} %bitcast.6, ...), custom_call_target="tpu_custom_call" | custom-call | tf_op jit(solution)/shard_map/attend/pallas_call | solution.py:277
  89.8 17.8 %send_back.1 = bf16[1,32,4096]{2,1,0:T(8,128)(2,1)S(1)} custom-call(bf16[4,2,4,32,128]{4,3,2,1,0:T(8,128)(2,1)S(1)} %bitcast.8), custom_call_target="tpu_custom_call" | custom-call | tf_op jit(solution)/shard_map/send_back/pallas_call | solution.py:342
  107.6 0.7 copy.11
Async XLA Ops:
  0.1 1.2 %copy-start = (bf16[4,32,4096]{2,1,0:T(8,128)(2,1)S(1)}, bf16[4,32,4096]{2,1,0:T(8,128)(2,1)}, u32[]{:S(2)}) copy-start(bf16[4,32,4096]{2,1,0:T(8,128)(2,1)} %ck_ref.1) | copy-start | bytes 3145732
  1.3 1.2 %copy-start.1 = (bf16[4,32,4096]{2,1,0:T(8,128)(2,1)S(1)}, bf16[4,32,4096]{2,1,0:T(8,128)(2,1)}, u32[]{:S(2)}) copy-start(bf16[4,32,4096]{2,1,0:T(8,128)(2,1)} %cv_ref.1) | copy-start | bytes 3145732
  2.5 0.9 copy-start.2
  3.5 0.9 copy-start.3
  4.4 0.9 copy-start.4
  67.0 0.7 copy-start.5
  67.7 0.7 copy-start.6
  68.3 0.7 copy-start.7
  69.0 0.7 copy-start.8

commit v2 on v0

v2 whole, which is shorter than its diff:
```python
import math

import jax
import jax.numpy as jnp
from jax import lax
from jax.experimental import pallas as pl
from jax.experimental.pallas import tpu as pltpu
from jax.sharding import PartitionSpec as P

HEADS = 32
HD = 128
ROWS = 32
NX, NY, NZ = 4, 4, 8
MESH = pl.DeviceIdType.MESH
BF = jnp.bfloat16
F32 = jnp.float32
FAR = 1e30
SCALE = math.log2(math.e) / math.sqrt(HD)

CK, CV, K, V, Q = range(5)

BEFORE = "y0 y1 y4 y2 y3 z0 z1 a0 z4 a1 z2 z3 q"
DURING = [
    "s00",
    "s10 b0",
    "b1 s01",
    "s11 d0 a2",
    "d1 s02",
    "s12 c0 a3",
    "c1 s03",
    "s13 b2",
    "b3 s20",
    "s30 d2",
    "d3 s21",
    "s31",
    "s22",
    "s32 c2",
    "c3 s23",
    "s33",
]


def place():
    slot, seq = lax.axis_index("slot"), lax.axis_index("seq")
    return seq // 16, (seq // 4) % 4, (slot // 2) * 4 + seq % 4, slot % 2


def device(x, y, z, core):
    return ((z // 4) * 2 + core, x * 16 + y * 4 + z % 4)


def wait_bytes(ref, sem):
    pltpu.make_async_copy(ref, ref, sem).wait()


def greet(peers):
    barrier = pltpu.get_barrier_semaphore()
    for peer in peers:
        pl.semaphore_signal(barrier, inc=1, device_id=peer, device_id_type=MESH)
    pl.semaphore_wait(barrier, len(peers))


def remote(src, dst, send, recv, peer):
    pltpu.make_async_remote_copy(
        src_ref=src, dst_ref=dst, send_sem=send, recv_sem=recv, device_id=peer, device_id_type=MESH
    ).start()


def local_copy(src, dst, sem):
    pltpu.make_async_copy(src, dst, sem).start()


def kernel(
    q_ref, k_ref, v_ref, ck_ref, cv_ref, rank_ref, level_ref, seen_ref, gate_ref, o_ref,
    rank, level, seen, gate, qb, kb, vb, sq, sk, sv, sck, scv, att, ret,
    scores, peak, acc, top, den,
    scalar_sem, y_send, y_recv, z_send, z_recv, x_send, x_recv, s_send, s_recv,
    back_send, back_recv,
):
    x, y, z, c = place()
    zl, zhi = z % 4, z // 4
    odd = z % 2
    head = y * NZ + z
    q_core = c + odd - 2 * c * odd
    step_x = 1 - 2 * c
    ahead = device((x + step_x + NX) % NX, y, z, c)
    behind = device((x - step_x + NX) % NX, y, z, c)
    other = device(x, y, z, 1 - c)

    small = ((rank_ref, rank), (level_ref, level), (seen_ref, seen), (gate_ref, gate))
    for n, (src, dst) in enumerate(small):
        local_copy(src, dst, scalar_sem.at[n])

    peers = [device(x, (y + d) % NY, z, c) for d in range(1, NY)]
    peers += [device(x, y, (z + d) % NZ, c) for d in range(1, NZ)]
    peers += [device(x, y, (z + d) % NZ, 1 - c) for d in range(NZ)]
    peers += [ahead, behind]
    greet(peers)

    pairs = [((z // 2 + e - c + 4) % 4) for e in range(2)]
    held = {Q: sq, K: sk, V: sv, CK: sck, CV: scv}
    given = {Q: q_ref, K: k_ref, V: v_ref, CK: ck_ref, CV: cv_ref}
    full = {CK: kb, K: kb, CV: vb, V: vb}

    def stage_y(n):
        for d in (1, 2, 3, 0):
            to = (y + d) % NY
            if n in (CK, CV):
                parts = [
                    (
                        given[n].at[
                            pl.ds(2 * c, 2), :,
                            pl.ds(pl.multiple_of(to * 1024 + pairs[e] * 256, 256), 256),
                        ],
                        held[n].at[e, :, y],
                    )
                    for e in range(2)
                ]
            else:
                columns = pl.ds(pl.multiple_of(to * 1024, 1024), 1024)
                parts = [(given[n].at[0, :, columns], held[n].at[y])]
            for src, dst in parts:
                if d:
                    remote(src, dst, y_send.at[n], y_recv.at[n], device(x, to, z, c))
                else:
                    local_copy(src, dst, y_recv.at[n])

    def stage_z(n):
        wait_bytes(held[n], y_recv.at[n])
        if n in (CK, CV):
            for e in range(2):
                for w in range(2):
                    to = pairs[e] * 2 + w
                    src = held[n].at[e, :, :, :, pl.ds(w * 128, 128)]
                    dst = full[n].at[0, 0, pl.ds(2, 2), zl]

                    @pl.when(to == z)
                    def _():
                        local_copy(src, dst, z_recv.at[n])

                    @pl.when(to != z)
                    def _():
                        remote(src, dst, z_send.at[n], z_recv.at[n], device(x, y, to, c))

            return
        for d in (4, 3, 5, 2, 6, 1, 7, 0):
            to = (z + d) % NZ
            src = held[n].at[:, :, pl.ds(pl.multiple_of(to * 128, 128), 128)]
            if n == Q:
                dst, core = qb.at[zhi * 2 + c, zl // 2], q_core
            else:
                dst, core = full[n].at[0, 0, zhi, zl], c
            if d:
                remote(src, dst, z_send.at[n], z_recv.at[n], device(x, y, to, core))
            elif n != Q:
                local_copy(src, dst, z_recv.at[n])
            else:

                @pl.when(odd == 0)
                def _():
                    local_copy(src, dst, z_recv.at[n])

                @pl.when(odd == 1)
                def _():
                    remote(src, dst, z_send.at[n], z_recv.at[n], other)

    def group(n, j, owner=0):
        return full[n].at[owner, j, pl.ds(2 if n in (CK, CV) else 0, 2)]

    def share(n, j):
        remote(group(n, j), group(n, j, 1), s_send.at[n, j], s_recv.at[n, j], other)

    def event(text):
        kind, n = text[0], int(text[1]) if len(text) > 1 else Q
        if kind == "y":
            stage_y(n)
        elif kind == "z":
            stage_z(n)
        elif kind == "q":
            wait_bytes(sq, z_recv.at[Q])
        elif kind == "a":
            wait_bytes(group(n, 0), z_recv.at[n])
            remote(group(n, 0), group(n, 1), x_send.at[n, 0], x_recv.at[n, 0], ahead)
            remote(group(n, 0), group(n, 2), x_send.at[n, 1], x_recv.at[n, 1], behind)
            share(n, 0)
        elif kind == "b":
            wait_bytes(group(n, 1), x_recv.at[n, 0])
            remote(group(n, 1), group(n, 3), x_send.at[n, 2], x_recv.at[n, 2], ahead)
            share(n, 1)
        elif kind == "d":
            wait_bytes(group(n, 2), x_recv.at[n, 1])
            share(n, 2)
        elif kind == "c":
            wait_bytes(group(n, 3), x_recv.at[n, 2])
            share(n, 3)
        else:
            j = int(text[2])
            wait_bytes(group(n, j, 1), s_recv.at[n, j])

    def matmul_scores(n, s, sub):
        keys = kb[n % 2, (n % 8) // 2, 2 * (1 - n // 8) + sub].reshape(512, HD)
        return lax.dot_general(
            keys, qb[s].reshape(256, HD), (((1,), (1,)), ((), ())), preferred_element_type=F32
        )

    def put_scores(buf, n, s, sub):
        tile = matmul_scores(n, s, sub)
        scores[buf, sub] = tile
        peak[buf, sub] = jnp.max(tile.reshape(64, 8, 256), axis=0)

    def step(n, s, after, after_s):
        buf = s % 2
        across = slice(s * 256, (s + 1) * 256)
        owner, in_flight = n % 2, n // 8
        holder = c + owner - 2 * c * owner
        shown = []
        for sub in range(2):
            span = rank[holder + 2 * sub] <= rank[s]
            cached = 2 * holder + sub < seen[s]
            shown.append(jnp.where(in_flight == 1, span.astype(jnp.int32), cached.astype(jnp.int32)) > 0)
        old = top[:, across]
        new = old
        for sub in range(2):
            most = jnp.max(peak[buf, sub], axis=0, keepdims=True) * SCALE
            new = jnp.maximum(new, jnp.where(shown[sub], most, -FAR))
        fade = jnp.exp2(old - new)
        total = jnp.zeros((HD, 256), F32)
        summed = jnp.zeros((8, 256), F32)
        for sub in range(2):
            put_scores(1 - buf, after, after_s, sub)
            shift = jnp.where(shown[sub], new, FAR)
            weights = jnp.exp2(scores[buf, sub] * SCALE - shift)
            summed = summed + jnp.sum(weights.reshape(64, 8, 256), axis=0)
            across_values = vb[owner, (n % 8) // 2, 2 * (1 - in_flight) + sub].reshape(512, HD).T
            total = total + lax.dot_general(
                across_values, weights.astype(BF), (((1,), (0,)), ((), ())),
                preferred_element_type=F32,
            )
        den[:, across] = den[:, across] * fade + summed
        acc[:, across] = acc[:, across] * fade + total
        top[:, across] = new

    for text in BEFORE.split():
        event(text)
    for n, (_, dst) in enumerate(small):
        wait_bytes(dst, scalar_sem.at[n])
    acc[...] = jnp.zeros_like(acc)
    den[...] = jnp.zeros_like(den)
    top[...] = jnp.full_like(top, -FAR)
    for sub in range(2):
        put_scores(0, 0, 0, sub)

    def item(n, carry):
        for m, texts in enumerate(DURING):

            @pl.when(n == m)
            def _():
                for text in texts.split():
                    event(text)

        for s in range(4):
            if s < 3:
                step(n, s, n, s + 1)
            else:
                step(n, s, jnp.minimum(n + 1, 15), 0)
        return carry

    lax.fori_loop(0, 16, item, 0)

    for s in range(4):
        across = slice(s * 256, (s + 1) * 256)
        gain = gate[level[s], head] / jnp.sum(den[:, across], axis=0, keepdims=True)
        att[s] = (acc[:, across] * gain).T.astype(BF).reshape(2, NY, ROWS, HD)
        span = (s + 1) % 4
        parity = (s % 2 + c) % 2
        for half in range(2):
            to = (span // 2) * 4 + 2 * half + parity
            itself = jnp.logical_and(to == z, c == span % 2)
            src = att.at[s, half]
            dst = ret.at[:, :, pl.ds(pl.multiple_of(z * 128, 128), 128)]

            @pl.when(itself)
            def _():
                local_copy(src, dst, back_recv.at[0])

            @pl.when(jnp.logical_not(itself))
            def _():
                remote(src, dst, back_send.at[0], back_recv.at[0], device(x, y, to, span % 2))

    wait_bytes(ret, back_recv.at[0])
    for d in (2, 1, 3, 0):
        to = (y + d) % NY
        src = ret.at[to]
        dst = o_ref.at[0, :, pl.ds(pl.multiple_of(y * 1024, 1024), 1024)]
        if d:
            remote(src, dst, back_send.at[1], back_recv.at[1], device(x, to, z, c))
        else:
            local_copy(src, dst, back_recv.at[1])

    for n in (CK, CV, K, V):
        for j in range(4):
            wait_bytes(group(n, j), s_send.at[n, j])
        for j in range(3):
            wait_bytes(group(n, j), x_send.at[n, j])
    for n in (Q, K, V):
        wait_bytes(held[n].at[pl.ds(0, 3)], y_send.at[n])
    for n in (CK, CV):
        wait_bytes(held[n].at[:, :, pl.ds(0, 3)], y_send.at[n])
        wait_bytes(held[n].at[:, :, pl.ds(0, 3)], z_send.at[n])
    for n in (K, V):
        wait_bytes(held[n].at[:, :, pl.ds(0, 896)], z_send.at[n])

    @pl.when(odd == 0)
    def _():
        wait_bytes(sq.at[:, :, pl.ds(0, 896)], z_send.at[Q])
        wait_bytes(ret, back_send.at[0])

    @pl.when(odd == 1)
    def _():
        wait_bytes(sq, z_send.at[Q])
        wait_bytes(ret.at[:, :, pl.ds(0, 896)], back_send.at[0])

    wait_bytes(ret.at[pl.ds(0, 3)], back_send.at[1])
    wait_bytes(o_ref, back_recv.at[1])


def local(*operands):
    dma = pltpu.SemaphoreType.DMA
    smem, vmem = pltpu.SMEM, pltpu.VMEM
    everything = (2, NX, 4, 4, NY, ROWS, HD)
    work = 4 * 1024 * 16384 * HD
    return pl.pallas_call(
        kernel,
        out_shape=jax.ShapeDtypeStruct((1, ROWS, HEADS * HD), BF),
        in_specs=[pl.BlockSpec(memory_space=pl.ANY)] * 9,
        out_specs=pl.BlockSpec(memory_space=pl.ANY),
        scratch_shapes=[
            smem((4,), jnp.int32), smem((4,), jnp.int32), smem((4,), jnp.int32), smem((16, 32), F32),
            vmem((4, 2, NY, ROWS, HD), BF), vmem(everything, BF), vmem(everything, BF),
            vmem((NY, ROWS, 1024), BF), vmem((NY, ROWS, 1024), BF), vmem((NY, ROWS, 1024), BF),
            vmem((2, 2, NY, ROWS, 256), BF), vmem((2, 2, NY, ROWS, 256), BF),
            vmem((4, 2, NY, ROWS, HD), BF), vmem((NY, ROWS, 1024), BF),
            vmem((2, 2, 512, 256), F32), vmem((2, 2, 8, 256), F32),
            vmem((HD, 1024), F32), vmem((1, 1024), F32), vmem((8, 1024), F32),
            dma((4,)), dma((5,)), dma((5,)), dma((5,)), dma((5,)),
            dma((4, 3)), dma((4, 3)), dma((4, 4)), dma((4, 4)), dma((2,)), dma((2,)),
        ],
        compiler_params=pltpu.CompilerParams(
            collective_id=0, has_side_effects=True, vmem_limit_bytes=56 * 2**20
        ),
        cost_estimate=pl.CostEstimate(
            flops=work, bytes_accessed=16 * 2**20, transcendentals=1024 * 16384
        ),
        name="attend_all",
    )(*operands)


def solution(mesh):
    own, cached = P("slot", "seq", None), P(None, "seq", None)
    placed = (own, own, own, cached, cached, P(), P(), P(), P())
    return jax.shard_map(local, mesh=mesh, in_specs=placed, out_specs=own, check_vma=False)
```

time: 312 us -> 83.1 us (0.27)
  blocking collectives: 139 us -> 0 us
  Pallas kernels: 0 us -> 80.2 us
  waiting for transfers between devices: 59.4 us -> 0 us
  matrix products: 45.6 us -> 0 us
  local copies, waits for them, and re-layouts: 26 us -> 1.67 us
  other arithmetic: 21.2 us -> 0 us
  between operations: 13.8 us -> 0.01 us
  starting transfers between devices: 5.64 us -> 0 us
    all_to_all x3 -> x0, blocking collectives: 139 us -> none  [the longest x1 78.1 us: local(): lax.all_to_all(spread(values, cache_values), 'seq', split_axis=2, concat_...]
    pallas_call x0 -> x1, Pallas kernels: none -> 80.2 us  [local(): pl.pallas_call(kernel, out_shape=jax.ShapeDtypeStruct((1, ROWS, HEADS * H...]
    all_gather x2 -> x0, waiting for transfers between devices: 48.2 us -> none  [the longest x1 48.2 us: local(): lax.all_gather(value_head, 'slot', axis=0, tiled=True)]
    dot_general x32 -> x0, matrix products: 45.6 us -> none  [the longest x16 23.6 us: one_block(): jnp.einsum('qhd,khd->hqk', query_block, key_rows, preferred_element_type=...]
    reduce_sum x21 -> x0, other arithmetic: 16.2 us -> none  [the longest x16 13.2 us: one_block(): block_sum = jnp.sum(weights, axis=-1)]
    ppermute x1 -> x0, waiting for transfers between devices: 11.2 us -> none  [passed_along(): return lax.ppermute(value, axis, pairs)]
    squeeze x2 -> x0, local copies, waits for them, and re-layouts: 7.47 us -> none  [the longest x1 3.8 us: local(): key_all[cached, 1]]
    another operation x25 -> x0, local copies, waits for them, and re-layouts: 5.99 us -> none
  transfers between devices with their start and end apart: 4 -> 0, of which waited for: 2 -> 0; matrix products, arithmetic and copies ran while one was open for 5% -> 0% of each run, Pallas kernels for 0% -> 0%
where the time goes in v2:
time: 83.1 us; the launch traced here: 81.9 us
  Pallas kernels  80.2 us (97%)
  local copies, waits for them, and re-layouts  1.67 us (2%)
    pallas_call x1, Pallas kernels, local(): pl.pallas_call(kernel, out_shape=jax.ShapeDtypeStruct((1, ROWS, HEADS * H...  80.2 us
    unnamed x1, local copies, waits for them, and re-layouts  1.67 us

profile of v2, /device:TPU:8, one launch (start us, length us, event | category | flops | bytes accessed | tf_op | source)
XLA Modules:
  0.0 81.9 jit_solution(16551043519180070412)
XLA Ops:
  0.0 80.2 %attend_all.1 = bf16[1,32,4096]{2,1,0:T(8,128)(2,1)} custom-call(bf16[1,32,4096]{2,1,0:T(8,128)(2,1)} %q_ref.1, bf16[1,32,4096]{2,1,0:T(8,128)(2,1)} %k_ref.1, bf16[1,32,4096]{2,1,0:T(8,128)(2,1)} %v_ref.1, bf16[4,32,4096]{2,1,0:T(8,128)(2,1)} %ck_ref.1, bf16[4,32,4096]{2,1,0:T(8,128)(2,1)} %cv_ref.1, s32[4]{0:T(128)} %rank_ref.1, s32[4]{0:T(128)} %level_ref.1, ...), custom_call_target="tpu_custom_call" | custom-call | flops 8589934592 | bytes 16777216 | tf_op jit(solution)/shard_map/attend_all/pallas_call | solution.py:332
  80.2 1.7 %copy.11 = bf16[1,32,4096]{2,1,0:T(8,128)(2,1)} copy(bf16[1,32,4096]{2,1,0:T(8,128)(2,1)} %attend_all.1) | data formatting | bytes 524288

commit v3 on v2

--- a/solution.py
+++ b/solution.py
@@ -18,26 +18,28 @@
 SCALE = math.log2(math.e) / math.sqrt(HD)
 
 CK, CV, K, V, Q = range(5)
-
-BEFORE = "y0 y1 y4 y2 y3 z0 z1 a0 z4 a1 z2 z3 q"
-DURING = [
-    "s00",
-    "s10 b0",
-    "b1 s01",
-    "s11 d0 a2",
-    "d1 s02",
-    "s12 c0 a3",
-    "c1 s03",
-    "s13 b2",
-    "b3 s20",
-    "s30 d2",
-    "d3 s21",
-    "s31",
-    "s22",
-    "s32 c2",
-    "c3 s23",
-    "s33",
-]
+UNITS = ((CK, 2, 1), (CK, 3, 1), (CV, 2, 2), (K, 0, 2), (V, 0, 2), (Q, 0, 2))
+QUERY = 5
+
+BEFORE = ("y0", "y1", "Z0", "Z1", "y2", "y3", "y4", "z0", "z1", "z2", "a0", "Y", "a1", "z3", "a2", "z4", "q")
+DURING = (
+    ("s00", "s10"),
+    ("b0", "b1", "s20"),
+    ("b2", "a3", "s01", "s11"),
+    ("d0", "d1", "s21"),
+    ("d2", "s02", "s12"),
+    ("c0", "c1", "a4", "s22"),
+    ("c2", "s03", "s13"),
+    ("s23",),
+    ("s30",),
+    ("b3", "s40",),
+    ("b4", "s31"),
+    ("d3", "s41"),
+    ("d4", "s32"),
+    ("c3", "s42"),
+    ("c4", "s33"),
+    ("s43",),
+)
 
 
 def place():
@@ -102,17 +104,18 @@
     given = {Q: q_ref, K: k_ref, V: v_ref, CK: ck_ref, CV: cv_ref}
     full = {CK: kb, K: kb, CV: vb, V: vb}
 
-    def stage_y(n):
+    def stage_y(u):
+        n, first, count = UNITS[u]
         for d in (1, 2, 3, 0):
             to = (y + d) % NY
             if n in (CK, CV):
                 parts = [
                     (
                         given[n].at[
-                            pl.ds(2 * c, 2), :,
+                            pl.ds(2 * c + first - 2, count), :,
                             pl.ds(pl.multiple_of(to * 1024 + pairs[e] * 256, 256), 256),
                         ],
-                        held[n].at[e, :, y],
+                        held[n].at[e, pl.ds(first - 2, count), y],
                     )
                     for e in range(2)
                 ]
@@ -121,81 +124,108 @@
                 parts = [(given[n].at[0, :, columns], held[n].at[y])]
             for src, dst in parts:
                 if d:
-                    remote(src, dst, y_send.at[n], y_recv.at[n], device(x, to, z, c))
+                    remote(src, dst, y_send.at[u], y_recv.at[u], device(x, to, z, c))
                 else:
-                    local_copy(src, dst, y_recv.at[n])
-
-    def stage_z(n):
-        wait_bytes(held[n], y_recv.at[n])
+                    local_copy(src, dst, y_recv.at[u])
+
+    def held_unit(u):
+        n, first, count = UNITS[u]
+        return held[n].at[:, pl.ds(first - 2, count)] if n in (CK, CV) else held[n]
+
+    def stage_z(u):
+        n, first, count = UNITS[u]
+        wait_bytes(held_unit(u), y_recv.at[u])
         if n in (CK, CV):
-            for e in range(2):
+            for e in (0, 1):
                 for w in range(2):
                     to = pairs[e] * 2 + w
-                    src = held[n].at[e, :, :, :, pl.ds(w * 128, 128)]
-                    dst = full[n].at[0, 0, pl.ds(2, 2), zl]
+                    src = held[n].at[e, pl.ds(first - 2, count), :, :, pl.ds(w * 128, 128)]
+                    dst = full[n].at[0, 0, pl.ds(first, count), zl]
 
                     @pl.when(to == z)
                     def _():
-                        local_copy(src, dst, z_recv.at[n])
+                        local_copy(src, dst, z_recv.at[u])
 
                     @pl.when(to != z)
                     def _():
-                        remote(src, dst, z_send.at[n], z_recv.at[n], device(x, y, to, c))
+                        remote(src, dst, z_send.at[u], z_recv.at[u], device(x, y, to, c))
 
             return
         for d in (4, 3, 5, 2, 6, 1, 7, 0):
             to = (z + d) % NZ
             src = held[n].at[:, :, pl.ds(pl.multiple_of(to * 128, 128), 128)]
-            if n == Q:
-                dst, core = qb.at[zhi * 2 + c, zl // 2], q_core
+            dst = full[n].at[0, 0, zhi, zl]
+            if d:
+                remote(src, dst, z_send.at[u], z_recv.at[u], device(x, y, to, c))
             else:
-                dst, core = full[n].at[0, 0, zhi, zl], c
+                local_copy(src, dst, z_recv.at[u])
+
+    def query_z(part):
+        for d in ((4, 3, 5, 2), (6, 1, 7, 0))[part]:
+            to = (z + d) % NZ
+            for row in range(NY):
+                src = q_ref.at[0, :, pl.ds(pl.multiple_of(row * 1024 + to * 128, 128), 128)]
+                dst = sq.at[row, zhi * 2 + c, zl // 2]
+                if d:
+                    remote(src, dst, z_send.at[QUERY], z_recv.at[QUERY], device(x, y, to, q_core))
+                else:
+
+                    @pl.when(odd == 0)
+                    def _():
+                        local_copy(src, dst, z_recv.at[QUERY])
+
+                    @pl.when(odd == 1)
+                    def _():
+                        remote(src, dst, z_send.at[QUERY], z_recv.at[QUERY], other)
+
+    def query_y():
+        wait_bytes(sq, z_recv.at[QUERY])
+        for d in (1, 2, 3, 0):
+            to = (y + d) % NY
+            dst = qb.at[:, :, y]
             if d:
-                remote(src, dst, z_send.at[n], z_recv.at[n], device(x, y, to, core))
-            elif n != Q:
-                local_copy(src, dst, z_recv.at[n])
+                remote(sq.at[to], dst, y_send.at[QUERY], y_recv.at[QUERY], device(x, to, z, c))
             else:
-
-                @pl.when(odd == 0)
-                def _():
-                    local_copy(src, dst, z_recv.at[n])
-
-                @pl.when(odd == 1)
-                def _():
-                    remote(src, dst, z_send.at[n], z_recv.at[n], other)
-
-    def group(n, j, owner=0):
-        return full[n].at[owner, j, pl.ds(2 if n in (CK, CV) else 0, 2)]
-
-    def share(n, j):
-        remote(group(n, j), group(n, j, 1), s_send.at[n, j], s_recv.at[n, j], other)
+                local_copy(sq.at[to], dst, y_recv.at[QUERY])
+
+    def group(u, j, owner=0):
+        n, first, count = UNITS[u]
+        return full[n].at[owner, j, pl.ds(first, count)]
+
+    def share(u, j):
+        remote(group(u, j), group(u, j, 1), s_send.at[u, j], s_recv.at[u, j], other)
 
     def event(text):
-        kind, n = text[0], int(text[1]) if len(text) > 1 else Q
+        kind = text[0]
+        u = int(text[1]) if len(text) > 1 else QUERY
         if kind == "y":
-            stage_y(n)
+            stage_y(u)
         elif kind == "z":
-            stage_z(n)
+            stage_z(u)
+        elif kind == "Z":
+            query_z(u)
+        elif kind == "Y":
+            query_y()
         elif kind == "q":
-            wait_bytes(sq, z_recv.at[Q])
+            wait_bytes(qb, y_recv.at[QUERY])
         elif kind == "a":
-            wait_bytes(group(n, 0), z_recv.at[n])
-            remote(group(n, 0), group(n, 1), x_send.at[n, 0], x_recv.at[n, 0], ahead)
-            remote(group(n, 0), group(n, 2), x_send.at[n, 1], x_recv.at[n, 1], behind)
-            share(n, 0)
+            wait_bytes(group(u, 0), z_recv.at[u])
+            remote(group(u, 0), group(u, 1), x_send.at[u, 0], x_recv.at[u, 0], ahead)
+            remote(group(u, 0), group(u, 2), x_send.at[u, 1], x_recv.at[u, 1], behind)
+            share(u, 0)
         elif kind == "b":
-            wait_bytes(group(n, 1), x_recv.at[n, 0])
-            remote(group(n, 1), group(n, 3), x_send.at[n, 2], x_recv.at[n, 2], ahead)
-            share(n, 1)
+            wait_bytes(group(u, 1), x_recv.at[u, 0])
+            remote(group(u, 1), group(u, 3), x_send.at[u, 2], x_recv.at[u, 2], ahead)
+            share(u, 1)
         elif kind == "d":
-            wait_bytes(group(n, 2), x_recv.at[n, 1])
-            share(n, 2)
+            wait_bytes(group(u, 2), x_recv.at[u, 1])
+            share(u, 2)
         elif kind == "c":
-            wait_bytes(group(n, 3), x_recv.at[n, 2])
-            share(n, 3)
+            wait_bytes(group(u, 3), x_recv.at[u, 2])
+            share(u, 3)
         else:
             j = int(text[2])
-            wait_bytes(group(n, j, 1), s_recv.at[n, j])
+            wait_bytes(group(u, j, 1), s_recv.at[u, j])
 
     def matmul_scores(n, s, sub):
         keys = kb[n % 2, (n % 8) // 2, 2 * (1 - n // 8) + sub].reshape(512, HD)
@@ -240,7 +270,7 @@
         acc[:, across] = acc[:, across] * fade + total
         top[:, across] = new
 
-    for text in BEFORE.split():
+    for text in BEFORE:
         event(text)
     for n, (_, dst) in enumerate(small):
         wait_bytes(dst, scalar_sem.at[n])
@@ -255,7 +285,7 @@
 
             @pl.when(n == m)
             def _():
-                for text in texts.split():
+                for text in texts:
                     event(text)
 
         for s in range(4):
@@ -297,27 +327,28 @@
         else:
             local_copy(src, dst, back_recv.at[1])
 
-    for n in (CK, CV, K, V):
+    for u in range(QUERY):
         for j in range(4):
-            wait_bytes(group(n, j), s_send.at[n, j])
+            wait_bytes(group(u, j), s_send.at[u, j])
         for j in range(3):
-            wait_bytes(group(n, j), x_send.at[n, j])
-    for n in (Q, K, V):
-        wait_bytes(held[n].at[pl.ds(0, 3)], y_send.at[n])
-    for n in (CK, CV):
-        wait_bytes(held[n].at[:, :, pl.ds(0, 3)], y_send.at[n])
-        wait_bytes(held[n].at[:, :, pl.ds(0, 3)], z_send.at[n])
-    for n in (K, V):
-        wait_bytes(held[n].at[:, :, pl.ds(0, 896)], z_send.at[n])
+            wait_bytes(group(u, j), x_send.at[u, j])
+        n, first, count = UNITS[u]
+        if n in (CK, CV):
+            for sem in (y_send, z_send):
+                wait_bytes(held[n].at[:, pl.ds(first - 2, count), pl.ds(0, 3)], sem.at[u])
+        else:
+            wait_bytes(held[n].at[pl.ds(0, 3)], y_send.at[u])
+            wait_bytes(held[n].at[:, :, pl.ds(0, 896)], z_send.at[u])
+    wait_bytes(sq.at[pl.ds(0, 3)], y_send.at[QUERY])
 
     @pl.when(odd == 0)
     def _():
-        wait_bytes(sq.at[:, :, pl.ds(0, 896)], z_send.at[Q])
+        wait_bytes(ret.at[:, :, pl.ds(0, 896)], z_send.at[QUERY])
         wait_bytes(ret, back_send.at[0])
 
     @pl.when(odd == 1)
     def _():
-        wait_bytes(sq, z_send.at[Q])
+        wait_bytes(ret, z_send.at[QUERY])
         wait_bytes(ret.at[:, :, pl.ds(0, 896)], back_send.at[0])
 
     wait_bytes(ret.at[pl.ds(0, 3)], back_send.at[1])
@@ -333,17 +364,17 @@
         kernel,
         out_shape=jax.ShapeDtypeStruct((1, ROWS, HEADS * HD), BF),
         in_specs=[pl.BlockSpec(memory_space=pl.ANY)] * 9,
-        out_specs=pl.BlockSpec(memory_space=pl.ANY),
+        out_specs=pl.BlockSpec(memory_space=pltpu.VMEM),
         scratch_shapes=[
             smem((4,), jnp.int32), smem((4,), jnp.int32), smem((4,), jnp.int32), smem((16, 32), F32),
             vmem((4, 2, NY, ROWS, HD), BF), vmem(everything, BF), vmem(everything, BF),
-            vmem((NY, ROWS, 1024), BF), vmem((NY, ROWS, 1024), BF), vmem((NY, ROWS, 1024), BF),
+            vmem((NY, 4, 2, ROWS, HD), BF), vmem((NY, ROWS, 1024), BF), vmem((NY, ROWS, 1024), BF),
             vmem((2, 2, NY, ROWS, 256), BF), vmem((2, 2, NY, ROWS, 256), BF),
             vmem((4, 2, NY, ROWS, HD), BF), vmem((NY, ROWS, 1024), BF),
             vmem((2, 2, 512, 256), F32), vmem((2, 2, 8, 256), F32),
             vmem((HD, 1024), F32), vmem((1, 1024), F32), vmem((8, 1024), F32),
-            dma((4,)), dma((5,)), dma((5,)), dma((5,)), dma((5,)),
-            dma((4, 3)), dma((4, 3)), dma((4, 4)), dma((4, 4)), dma((2,)), dma((2,)),
+            dma((4,)), dma((6,)), dma((6,)), dma((6,)), dma((6,)),
+            dma((5, 3)), dma((5, 3)), dma((5, 4)), dma((5, 4)), dma((2,)), dma((2,)),
         ],
         compiler_params=pltpu.CompilerParams(
             collective_id=0, has_side_effects=True, vmem_limit_bytes=56 * 2**20

time: 83.1 us -> 76.3 us (0.918); the launches traced: 81.9 us -> 76.2 us
  Pallas kernels: 80.2 us -> 74.5 us
    pallas_call x1, Pallas kernels: 80.2 us -> 74.5 us  [local(): pl.pallas_call(kernel, out_shape=jax.ShapeDtypeStruct((1, ROWS, HEADS * H...]
where the time goes in v3:
time: 76.3 us; the launch traced here: 76.2 us
  Pallas kernels  74.5 us (98%)
  local copies, waits for them, and re-layouts  1.67 us (2%)
    pallas_call x1, Pallas kernels, local(): pl.pallas_call(kernel, out_shape=jax.ShapeDtypeStruct((1, ROWS, HEADS * H...  74.5 us
    unnamed x1, local copies, waits for them, and re-layouts  1.67 us

profile of v3, /device:TPU:8, one launch (start us, length us, event | category | flops | bytes accessed | tf_op | source)
XLA Modules:
  0.0 76.2 jit_solution(5670418367529638973)
XLA Ops:
  0.0 74.5 %attend_all.1 = bf16[1,32,4096]{2,1,0:T(8,128)(2,1)} custom-call(bf16[1,32,4096]{2,1,0:T(8,128)(2,1)} %q_ref.1, bf16[1,32,4096]{2,1,0:T(8,128)(2,1)} %k_ref.1, bf16[1,32,4096]{2,1,0:T(8,128)(2,1)} %v_ref.1, bf16[4,32,4096]{2,1,0:T(8,128)(2,1)} %ck_ref.1, bf16[4,32,4096]{2,1,0:T(8,128)(2,1)} %cv_ref.1, s32[4]{0:T(128)} %rank_ref.1, s32[4]{0:T(128)} %level_ref.1, ...), custom_call_target="tpu_custom_call" | custom-call | flops 8589934592 | bytes 16777216 | tf_op jit(solution)/shard_map/attend_all/pallas_call | solution.py:363
  74.5 1.7 %copy.11 = bf16[1,32,4096]{2,1,0:T(8,128)(2,1)} copy(bf16[1,32,4096]{2,1,0:T(8,128)(2,1)} %attend_all.1) | data formatting | bytes 524288

commit v4 on v3

--- a/solution.py
+++ b/solution.py
@@ -74,7 +74,7 @@
 
 def kernel(
     q_ref, k_ref, v_ref, ck_ref, cv_ref, rank_ref, level_ref, seen_ref, gate_ref, o_ref,
-    rank, level, seen, gate, qb, kb, vb, sq, sk, sv, sck, scv, att, ret,
+    rank, level, seen, gate, qb, kb, vb, sq, sk, sv, sck, scv, att,
     scores, peak, acc, top, den,
     scalar_sem, y_send, y_recv, z_send, z_recv, x_send, x_recv, s_send, s_recv,
     back_send, back_recv,
@@ -297,6 +297,7 @@
 
     lax.fori_loop(0, 16, item, 0)
 
+    columns = pl.ds(pl.multiple_of(head * HD, HD), HD)
     for s in range(4):
         across = slice(s * 256, (s + 1) * 256)
         gain = gate[level[s], head] / jnp.sum(den[:, across], axis=0, keepdims=True)
@@ -306,26 +307,21 @@
         for half in range(2):
             to = (span // 2) * 4 + 2 * half + parity
             itself = jnp.logical_and(to == z, c == span % 2)
-            src = att.at[s, half]
-            dst = ret.at[:, :, pl.ds(pl.multiple_of(z * 128, 128), 128)]
-
-            @pl.when(itself)
-            def _():
-                local_copy(src, dst, back_recv.at[0])
-
-            @pl.when(jnp.logical_not(itself))
-            def _():
-                remote(src, dst, back_send.at[0], back_recv.at[0], device(x, y, to, span % 2))
-
-    wait_bytes(ret, back_recv.at[0])
-    for d in (2, 1, 3, 0):
-        to = (y + d) % NY
-        src = ret.at[to]
-        dst = o_ref.at[0, :, pl.ds(pl.multiple_of(y * 1024, 1024), 1024)]
-        if d:
-            remote(src, dst, back_send.at[1], back_recv.at[1], device(x, to, z, c))
-        else:
-            local_copy(src, dst, back_recv.at[1])
+            dst = o_ref.at[0, :, columns]
+            for d in (2, 1, 3, 0):
+                row = (y + d) % NY
+                src = att.at[s, half, row]
+                if d:
+                    remote(src, dst, back_send, back_recv, device(x, row, to, span % 2))
+                else:
+
+                    @pl.when(itself)
+                    def _():
+                        local_copy(src, dst, back_recv)
+
+                    @pl.when(jnp.logical_not(itself))
+                    def _():
+                        remote(src, dst, back_send, back_recv, device(x, y, to, span % 2))
 
     for u in range(QUERY):
         for j in range(4):
@@ -343,16 +339,15 @@
 
     @pl.when(odd == 0)
     def _():
-        wait_bytes(ret.at[:, :, pl.ds(0, 896)], z_send.at[QUERY])
-        wait_bytes(ret, back_send.at[0])
+        wait_bytes(sk.at[:, :, pl.ds(0, 896)], z_send.at[QUERY])
+        wait_bytes(att, back_send)
 
     @pl.when(odd == 1)
     def _():
-        wait_bytes(ret, z_send.at[QUERY])
-        wait_bytes(ret.at[:, :, pl.ds(0, 896)], back_send.at[0])
-
-    wait_bytes(ret.at[pl.ds(0, 3)], back_send.at[1])
-    wait_bytes(o_ref, back_recv.at[1])
+        wait_bytes(sk, z_send.at[QUERY])
+        wait_bytes(o_ref.at[:, :, pl.ds(0, 31 * HD)], back_send)
+
+    wait_bytes(o_ref, back_recv)
 
 
 def local(*operands):
@@ -370,11 +365,11 @@
             vmem((4, 2, NY, ROWS, HD), BF), vmem(everything, BF), vmem(everything, BF),
             vmem((NY, 4, 2, ROWS, HD), BF), vmem((NY, ROWS, 1024), BF), vmem((NY, ROWS, 1024), BF),
             vmem((2, 2, NY, ROWS, 256), BF), vmem((2, 2, NY, ROWS, 256), BF),
-            vmem((4, 2, NY, ROWS, HD), BF), vmem((NY, ROWS, 1024), BF),
+            vmem((4, 2, NY, ROWS, HD), BF),
             vmem((2, 2, 512, 256), F32), vmem((2, 2, 8, 256), F32),
             vmem((HD, 1024), F32), vmem((1, 1024), F32), vmem((8, 1024), F32),
             dma((4,)), dma((6,)), dma((6,)), dma((6,)), dma((6,)),
-            dma((5, 3)), dma((5, 3)), dma((5, 4)), dma((5, 4)), dma((2,)), dma((2,)),
+            dma((5, 3)), dma((5, 3)), dma((5, 4)), dma((5, 4)), dma, dma,
         ],
         compiler_params=pltpu.CompilerParams(
             collective_id=0, has_side_effects=True, vmem_limit_bytes=56 * 2**20

time: 76.3 us -> 72.6 us (0.952)
  Pallas kernels: 74.5 us -> 70.7 us
    pallas_call x1, Pallas kernels: 74.5 us -> 70.7 us  [local(): pl.pallas_call(kernel, out_shape=jax.ShapeDtypeStruct((1, ROWS, HEADS * H...]
where the time goes in v4:
time: 72.6 us; the launch traced here: 72.4 us
  Pallas kernels  70.7 us (97%)
  local copies, waits for them, and re-layouts  1.67 us (2%)
    pallas_call x1, Pallas kernels, local(): pl.pallas_call(kernel, out_shape=jax.ShapeDtypeStruct((1, ROWS, HEADS * H...  70.7 us
    unnamed x1, local copies, waits for them, and re-layouts  1.67 us

profile of v4, /device:TPU:8, one launch (start us, length us, event | category | flops | bytes accessed | tf_op | source)
XLA Modules:
  0.0 72.4 jit_solution(779102197598743267)
XLA Ops:
  0.0 70.7 %attend_all.1 = bf16[1,32,4096]{2,1,0:T(8,128)(2,1)} custom-call(bf16[1,32,4096]{2,1,0:T(8,128)(2,1)} %q_ref.1, bf16[1,32,4096]{2,1,0:T(8,128)(2,1)} %k_ref.1, bf16[1,32,4096]{2,1,0:T(8,128)(2,1)} %v_ref.1, bf16[4,32,4096]{2,1,0:T(8,128)(2,1)} %ck_ref.1, bf16[4,32,4096]{2,1,0:T(8,128)(2,1)} %cv_ref.1, s32[4]{0:T(128)} %rank_ref.1, s32[4]{0:T(128)} %level_ref.1, ...), custom_call_target="tpu_custom_call" | custom-call | flops 8589934592 | bytes 16777216 | tf_op jit(solution)/shard_map/attend_all/pallas_call | solution.py:358
  70.7 1.7 %copy.11 = bf16[1,32,4096]{2,1,0:T(8,128)(2,1)} copy(bf16[1,32,4096]{2,1,0:T(8,128)(2,1)} %attend_all.1) | data formatting | bytes 524288

commit v5 on v4

--- a/solution.py
+++ b/solution.py
@@ -21,7 +21,9 @@
 UNITS = ((CK, 2, 1), (CK, 3, 1), (CV, 2, 2), (K, 0, 2), (V, 0, 2), (Q, 0, 2))
 QUERY = 5
 
-BEFORE = ("y0", "y1", "Z0", "Z1", "y2", "y3", "y4", "z0", "z1", "z2", "a0", "Y", "a1", "z3", "a2", "z4", "q")
+BEFORE = (
+    "y0", "y1", "Z0", "y2", "y3", "y4", "z0", "Z1", "z1", "z2", "a0", "Y", "a1", "z3", "a2", "z4", "q",
+)
 DURING = (
     ("s00", "s10"),
     ("b0", "b1", "s20"),
@@ -281,7 +283,7 @@
         put_scores(0, 0, 0, sub)
 
     def item(n, carry):
-        for m, texts in enumerate(DURING):
+        for m, texts in enumerate(DURING[:15]):
 
             @pl.when(n == m)
             def _():
@@ -289,16 +291,16 @@
                     event(text)
 
         for s in range(4):
-            if s < 3:
-                step(n, s, n, s + 1)
-            else:
-                step(n, s, jnp.minimum(n + 1, 15), 0)
+            step(n, s, n + s // 3, (s + 1) % 4)
         return carry
 
-    lax.fori_loop(0, 16, item, 0)
+    lax.fori_loop(0, 15, item, 0)
+    for text in DURING[15]:
+        event(text)
 
     columns = pl.ds(pl.multiple_of(head * HD, HD), HD)
     for s in range(4):
+        step(15, s, 15, min(s + 1, 3))
         across = slice(s * 256, (s + 1) * 256)
         gain = gate[level[s], head] / jnp.sum(den[:, across], axis=0, keepdims=True)
         att[s] = (acc[:, across] * gain).T.astype(BF).reshape(2, NY, ROWS, HD)
@@ -359,7 +361,7 @@
         kernel,
         out_shape=jax.ShapeDtypeStruct((1, ROWS, HEADS * HD), BF),
         in_specs=[pl.BlockSpec(memory_space=pl.ANY)] * 9,
-        out_specs=pl.BlockSpec(memory_space=pltpu.VMEM),
+        out_specs=pl.BlockSpec(memory_space=pl.ANY),
         scratch_shapes=[
             smem((4,), jnp.int32), smem((4,), jnp.int32), smem((4,), jnp.int32), smem((16, 32), F32),
             vmem((4, 2, NY, ROWS, HD), BF), vmem(everything, BF), vmem(everything, BF),

time: 72.6 us -> 70.8 us (0.975)
  Pallas kernels: 70.7 us -> 68.2 us
    pallas_call x1, Pallas kernels: 70.7 us -> 68.2 us  [local(): pl.pallas_call(kernel, out_shape=jax.ShapeDtypeStruct((1, ROWS, HEADS * H...]
where the time goes in v5:
time: 70.8 us; the launch traced here: 69.9 us
  Pallas kernels  68.2 us (96%)
  local copies, waits for them, and re-layouts  1.67 us (2%)
    pallas_call x1, Pallas kernels, local(): pl.pallas_call(kernel, out_shape=jax.ShapeDtypeStruct((1, ROWS, HEADS * H...  68.2 us
    unnamed x1, local copies, waits for them, and re-layouts  1.67 us

profile of v5, /device:TPU:8, one launch (start us, length us, event | category | flops | bytes accessed | tf_op | source)
XLA Modules:
  0.0 69.9 jit_solution(11902505742034219564)
XLA Ops:
  0.0 68.2 %attend_all.1 = bf16[1,32,4096]{2,1,0:T(8,128)(2,1)} custom-call(bf16[1,32,4096]{2,1,0:T(8,128)(2,1)} %q_ref.1, bf16[1,32,4096]{2,1,0:T(8,128)(2,1)} %k_ref.1, bf16[1,32,4096]{2,1,0:T(8,128)(2,1)} %v_ref.1, bf16[4,32,4096]{2,1,0:T(8,128)(2,1)} %ck_ref.1, bf16[4,32,4096]{2,1,0:T(8,128)(2,1)} %cv_ref.1, s32[4]{0:T(128)} %rank_ref.1, s32[4]{0:T(128)} %level_ref.1, ...), custom_call_target="tpu_custom_call" | custom-call | flops 8589934592 | bytes 16777216 | tf_op jit(solution)/shard_map/attend_all/pallas_call | solution.py:360
  68.2 1.7 %copy.11 = bf16[1,32,4096]{2,1,0:T(8,128)(2,1)} copy(bf16[1,32,4096]{2,1,0:T(8,128)(2,1)} %attend_all.1) | data formatting | bytes 524288

commit v6 on v5

--- a/solution.py
+++ b/solution.py
@@ -95,9 +95,9 @@
     for n, (src, dst) in enumerate(small):
         local_copy(src, dst, scalar_sem.at[n])
 
-    peers = [device(x, (y + d) % NY, z, c) for d in range(1, NY)]
-    peers += [device(x, y, (z + d) % NZ, c) for d in range(1, NZ)]
-    peers += [device(x, y, (z + d) % NZ, 1 - c) for d in range(NZ)]
+    peers = [device(x, y, (z + d) % NZ, c) for d in (4, 3, 5, 2, 6, 1, 7)]
+    peers += [device(x, y, (z + d) % NZ, 1 - c) for d in (4, 3, 5, 2, 6, 1, 7, 0)]
+    peers += [device(x, (y + d) % NY, z, c) for d in (2, 1, 3)]
     peers += [ahead, behind]
     greet(peers)
 
@@ -309,7 +309,7 @@
         for half in range(2):
             to = (span // 2) * 4 + 2 * half + parity
             itself = jnp.logical_and(to == z, c == span % 2)
-            dst = o_ref.at[0, :, columns]
+            dst = o_ref.at[head]
             for d in (2, 1, 3, 0):
                 row = (y + d) % NY
                 src = att.at[s, half, row]
@@ -347,7 +347,7 @@
     @pl.when(odd == 1)
     def _():
         wait_bytes(sk, z_send.at[QUERY])
-        wait_bytes(o_ref.at[:, :, pl.ds(0, 31 * HD)], back_send)
+        wait_bytes(o_ref.at[pl.ds(0, 31)], back_send)
 
     wait_bytes(o_ref, back_recv)
 
@@ -357,9 +357,9 @@
     smem, vmem = pltpu.SMEM, pltpu.VMEM
     everything = (2, NX, 4, 4, NY, ROWS, HD)
     work = 4 * 1024 * 16384 * HD
-    return pl.pallas_call(
+    heads = pl.pallas_call(
         kernel,
-        out_shape=jax.ShapeDtypeStruct((1, ROWS, HEADS * HD), BF),
+        out_shape=jax.ShapeDtypeStruct((HEADS, ROWS, HD), BF),
         in_specs=[pl.BlockSpec(memory_space=pl.ANY)] * 9,
         out_specs=pl.BlockSpec(memory_space=pl.ANY),
         scratch_shapes=[
@@ -381,6 +381,7 @@
         ),
         name="attend_all",
     )(*operands)
+    return heads.transpose(1, 0, 2).reshape(1, ROWS, HEADS * HD)
 
 
 def solution(mesh):

time: 70.8 us -> 70.7 us (level)
    unnamed x1 -> x0, local copies, waits for them, and re-layouts: 1.67 us -> none
    transpose x0 -> x1, local copies, waits for them, and re-layouts: none -> 1.06 us  [local(): return heads.transpose(1, 0, 2).reshape(1, ROWS, HEADS * HD)]
    reshape x0 -> x1, local copies, waits for them, and re-layouts: none -> 0.82 us  [local(): return heads.transpose(1, 0, 2).reshape(1, ROWS, HEADS * HD)]
where the time goes in v6:
time: 70.7 us; the launch traced here: 70.2 us
  Pallas kernels  68.3 us (97%)
  local copies, waits for them, and re-layouts  1.87 us (3%)
    pallas_call x1, Pallas kernels, local(): pl.pallas_call(kernel, out_shape=jax.ShapeDtypeStruct((HEADS, ROWS, HD),...  68.3 us

profile of v6, /device:TPU:8, one launch (start us, length us, event | category | flops | bytes accessed | tf_op | source)
XLA Modules:
  0.0 70.2 jit_solution(320636543367822794)
XLA Ops:
  0.0 68.3 %attend_all.1 = bf16[32,32,128]{2,1,0:T(8,128)(2,1)} custom-call(bf16[1,32,4096]{2,1,0:T(8,128)(2,1)} %q_ref.1, bf16[1,32,4096]{2,1,0:T(8,128)(2,1)} %k_ref.1, bf16[1,32,4096]{2,1,0:T(8,128)(2,1)} %v_ref.1, bf16[4,32,4096]{2,1,0:T(8,128)(2,1)} %ck_ref.1, bf16[4,32,4096]{2,1,0:T(8,128)(2,1)} %cv_ref.1, s32[4]{0:T(128)} %rank_ref.1, s32[4]{0:T(128)} %level_ref.1, ...), custom_call_target="tpu_custom_call" | custom-call | flops 8589934592 | bytes 16777216 | tf_op jit(solution)/shard_map/attend_all/pallas_call | solution.py:360
  68.3 1.1 %copy.10 = bf16[32,32,128]{2,1,0:T(8,128)(2,1)S(1)} copy(bf16[32,32,128]{2,0,1:T(8,128)(2,1)} %bitcast.1) | data formatting | bytes 524288 | tf_op jit(solution)/shard_map/transpose | solution.py:384
  69.4 0.8 %reshape.3 = bf16[1,32,4096]{2,1,0:T(8,128)(2,1)} reshape(bf16[32,32,128]{2,1,0:T(8,128)(2,1)S(1)} %copy.10) | data formatting | bytes 524288 | tf_op jit(solution)/shard_map/reshape | solution.py:384

commit v7 on v6

--- a/solution.py
+++ b/solution.py
@@ -259,7 +259,8 @@
         total = jnp.zeros((HD, 256), F32)
         summed = jnp.zeros((8, 256), F32)
         for sub in range(2):
-            put_scores(1 - buf, after, after_s, sub)
+            if after is not None:
+                put_scores(1 - buf, after, after_s, sub)
             shift = jnp.where(shown[sub], new, FAR)
             weights = jnp.exp2(scores[buf, sub] * SCALE - shift)
             summed = summed + jnp.sum(weights.reshape(64, 8, 256), axis=0)
@@ -300,7 +301,7 @@
 
     columns = pl.ds(pl.multiple_of(head * HD, HD), HD)
     for s in range(4):
-        step(15, s, 15, min(s + 1, 3))
+        step(15, s, 15 if s < 3 else None, s + 1)
         across = slice(s * 256, (s + 1) * 256)
         gain = gate[level[s], head] / jnp.sum(den[:, across], axis=0, keepdims=True)
         att[s] = (acc[:, across] * gain).T.astype(BF).reshape(2, NY, ROWS, HD)

time: 70.7 us -> 70.7 us (level)
  no operation moved by 1% of the time
where the time goes in v7:
time: 70.7 us; the launch traced here: 70.2 us
  Pallas kernels  68.3 us (97%)
  local copies, waits for them, and re-layouts  1.87 us (3%)
    pallas_call x1, Pallas kernels, local(): pl.pallas_call(kernel, out_shape=jax.ShapeDtypeStruct((HEADS, ROWS, HD),...  68.3 us

profile of v7, /device:TPU:8, one launch (start us, length us, event | category | flops | bytes accessed | tf_op | source)
XLA Modules:
  0.0 70.2 jit_solution(14689690249700648719)
XLA Ops:
  0.0 68.3 %attend_all.1 = bf16[32,32,128]{2,1,0:T(8,128)(2,1)} custom-call(bf16[1,32,4096]{2,1,0:T(8,128)(2,1)} %q_ref.1, bf16[1,32,4096]{2,1,0:T(8,128)(2,1)} %k_ref.1, bf16[1,32,4096]{2,1,0:T(8,128)(2,1)} %v_ref.1, bf16[4,32,4096]{2,1,0:T(8,128)(2,1)} %ck_ref.1, bf16[4,32,4096]{2,1,0:T(8,128)(2,1)} %cv_ref.1, s32[4]{0:T(128)} %rank_ref.1, s32[4]{0:T(128)} %level_ref.1, ...), custom_call_target="tpu_custom_call" | custom-call | flops 8589934592 | bytes 16777216 | tf_op jit(solution)/shard_map/attend_all/pallas_call | solution.py:361
  68.3 1.1 %copy.10 = bf16[32,32,128]{2,1,0:T(8,128)(2,1)S(1)} copy(bf16[32,32,128]{2,0,1:T(8,128)(2,1)} %bitcast.1) | data formatting | bytes 524288 | tf_op jit(solution)/shard_map/transpose | solution.py:385
  69.4 0.8 %reshape.3 = bf16[1,32,4096]{2,1,0:T(8,128)(2,1)} reshape(bf16[32,32,128]{2,1,0:T(8,128)(2,1)S(1)} %copy.10) | data formatting | bytes 524288 | tf_op jit(solution)/shard_map/reshape | solution.py:385
